TPU v7x, 128 devices: a whole 4x4x4 slice. The times are simulated.
128 devices in a mesh: dp: 16 (over z, x_lo, core), mp: 8 (over y, x_hi).
Axes of the slice: x: 4 (x_hi: 2, x_lo: 2; x = x_hi * 2 + x_lo), y: 4, z: 4, core: 2. Of those that a mesh axis runs over, the one named last changes fastest.
Arguments:
- tokens: bfloat16 [16384, 2048], P(('dp', 'mp')), may hold values from -24 to 24
- cotangent: bfloat16 [16384, 2048], P(('dp', 'mp')), may hold values from -24 to 24
- seq_lengths: int32 [16, 4], P('dp'), may hold values from 0 to 1024, as said below
- w_qkv: bfloat16 [2048, 3, 2048], P('dp', None, 'mp'), may hold values from -0.125 to 0.125
- b_qkv: float32 [3, 2048], P(None, 'mp'), may hold values from -1.75 to 1.75
- w_out: bfloat16 [2048, 2048], P('mp', 'dp'), may hold values from -0.75 to 0.75
- b_out: float32 [2048], replicated, may hold values from -1.75 to 1.75
- w_fc1: bfloat16 [2048, 8192], P('dp', 'mp'), may hold values from -0.125 to 0.125
- b_fc1: float32 [8192], P('mp'), may hold values from -3 to 3
- w_fc2: bfloat16 [8192, 2048], P('mp', 'dp'), may hold values from -0.0625 to 0.0625
- b_fc2: float32 [2048], replicated, may hold values from -1.75 to 1.75
- ln_gain: float32 [2048], replicated, may hold values from 0.1 to 1.9
- ln_bias: float32 [2048], replicated, may hold values from -1.75 to 1.75
Outputs:
- mixed: bfloat16 [16384, 2048], P(('dp', 'mp'))
- tokens_grad: bfloat16 [16384, 2048], P(('dp', 'mp'))
- w_qkv_grad: float32 [2048, 3, 2048], P('dp', None, 'mp')
- b_qkv_grad: float32 [3, 2048], P(None, 'mp')
- w_out_grad: float32 [2048, 2048], P('mp', 'dp')
- b_out_grad: float32 [2048], replicated
- w_fc1_grad: float32 [2048, 8192], P('dp', 'mp')
- b_fc1_grad: float32 [8192], P('mp')
- w_fc2_grad: float32 [8192, 2048], P('mp', 'dp')
- b_fc2_grad: float32 [2048], replicated
- ln_gain_grad: float32 [2048], replicated
- ln_bias_grad: float32 [2048], replicated
Inputs may be any that keep to these rules, and one draw needn't show every extreme that they name: `seq_lengths`: the four lengths of a data group add up to 1024; a length may be 0. The second sequence starts within the group's first 128 rows and ends within its last 128; in some group it holds all 1024 rows.
All inputs are finite; a program needn't handle non-finite values.
Results may differ from a plain program's by a relative error of at most 0.018.
Values may be sent and summed in bfloat16 or wider, within the bound.
A program may use at most 128 MiB of HBM per device.

v0:
```python
import jax
import jax.numpy as jnp
from jax import lax
from jax.sharding import PartitionSpec as P

HD = 64
ROT = 32


def in_blocks(shard, dim, devices):
    before, after = (shard.shape[:dim], shard.shape[dim + 1 :])
    return jnp.moveaxis(shard.reshape(*before, devices, -1, *after), dim, 0)


def summed_on_arrival(shard, axis, dim):
    tiles = in_blocks(shard, dim, lax.axis_size(axis))
    arrived = lax.all_to_all(tiles, axis, split_axis=0, concat_axis=0, tiled=True)
    return arrived.astype(jnp.float32).sum(axis=0)


def normalize(values, gain_vec, shift_vec):
    center = values - jnp.mean(values, axis=-1, keepdims=True)
    spread = jnp.mean(center * center, axis=-1, keepdims=True)
    return center * lax.rsqrt(spread + 1e-05) * gain_vec + shift_vec


def rotary(heads, places):
    half_rot = ROT // 2
    freqs = 10000.0 ** (-2.0 * jnp.arange(half_rot, dtype=jnp.float32) / ROT)
    angles = places[:, None] * freqs[None, :]
    cosine = jnp.cos(angles)[:, None, :]
    sine = jnp.sin(angles)[:, None, :]
    first_half = heads[..., :half_rot]
    second_half = heads[..., half_rot:ROT]
    return jnp.concatenate(
        [
            first_half * cosine - second_half * sine,
            second_half * cosine + first_half * sine,
            heads[..., ROT:],
        ],
        axis=-1,
    )


def layout(lengths, total_rows):
    ends = jnp.cumsum(lengths)
    starts = ends - lengths
    row_ids = jnp.arange(total_rows, dtype=jnp.int32)
    segment = jnp.sum((row_ids[:, None] >= ends[None, :3]).astype(jnp.int32), axis=1)
    slots = jnp.arange(4, dtype=jnp.int32)
    begin = jnp.sum(jnp.where(segment[:, None] == slots[None, :], starts[None, :], 0), axis=1)
    return (row_ids, segment, row_ids - begin)


def gelu_tanh(pre_act):
    return jax.nn.gelu(pre_act, approximate=True)


def per_device(
    tokens,
    cotangent,
    seq_lengths,
    w_qkv,
    b_qkv,
    w_out,
    b_out,
    w_fc1,
    b_fc1,
    w_fc2,
    b_fc2,
    ln_gain,
    ln_bias,
):
    shard_rows = tokens.shape[0]
    group_rows = shard_rows * lax.axis_size("mp")
    local_width = b_qkv.shape[1]
    local_heads = local_width // HD
    block_rows = min(512, group_rows)
    block_count = group_rows // block_rows
    scale = HD ** (-0.5)
    inputs32 = tokens.astype(jnp.float32)
    normed, norm_back = jax.vjp(normalize, inputs32, ln_gain, ln_bias)
    weights = (
        lax.all_gather(w_qkv, "dp", axis=0, tiled=True),
        lax.all_gather(w_out, "dp", axis=1, tiled=True),
        lax.all_gather(w_fc1, "dp", axis=0, tiled=True),
        lax.all_gather(w_fc2, "dp", axis=1, tiled=True),
    )
    qkv_full, out_full, up_full, down_full = weights
    normed_all = lax.all_gather(normed.astype(jnp.bfloat16), "mp", axis=0, tiled=True)
    row_ids, segment, places = layout(seq_lengths[0], group_rows)
    angle_pos = places.astype(jnp.float32)
    mixed_qkv = (
        jnp.einsum("gd,dte->gte", normed_all, qkv_full, preferred_element_type=jnp.float32)
        + b_qkv[None]
    )
    shaped = mixed_qkv.reshape(group_rows, 3, local_heads, HD)
    query_rot, query_back = jax.vjp(lambda heads: rotary(heads, angle_pos), shaped[:, 0])
    key_rot, key_back = jax.vjp(lambda heads: rotary(heads, angle_pos), shaped[:, 1])
    queries = query_rot.astype(jnp.bfloat16)
    keys_all = key_rot.astype(jnp.bfloat16)
    values_all = shaped[:, 2].astype(jnp.bfloat16)
    query_blocks = queries.reshape(block_count, block_rows, local_heads, HD)
    seg_blocks = segment.reshape(block_count, block_rows)
    row_blocks = row_ids.reshape(block_count, block_rows)

    def masked_scores(query_blk, seg_blk, row_blk):
        scores = (
            jnp.einsum("qhd,khd->hqk", query_blk, keys_all, preferred_element_type=jnp.float32)
            * scale
        )
        allowed = (seg_blk[:, None] == segment[None, :]) & (row_ids[None, :] <= row_blk[:, None])
        return jnp.where(allowed[None], scores, -1e30)

    def forward_block(operands):
        query_blk, seg_blk, row_blk = operands
        scores = masked_scores(query_blk, seg_blk, row_blk)
        peak = jnp.max(scores, axis=-1, keepdims=True)
        expo = jnp.exp(scores - peak)
        totals = jnp.sum(expo, axis=-1, keepdims=True)
        probs_low = (expo / totals).astype(jnp.bfloat16)
        attended = jnp.einsum(
            "hqk,khd->qhd", probs_low, values_all, preferred_element_type=jnp.float32
        )
        return (
            attended.astype(jnp.bfloat16).reshape(block_rows, local_width),
            (peak + jnp.log(totals))[..., 0],
        )

    attended_blocks, log_totals = lax.map(forward_block, (query_blocks, seg_blocks, row_blocks))
    attended_all = attended_blocks.reshape(group_rows, local_width)
    hidden_pre = jnp.dot(normed_all, up_full, preferred_element_type=jnp.float32) + b_fc1
    hidden_act, gelu_back = jax.vjp(gelu_tanh, hidden_pre)
    hidden_all = hidden_act.astype(jnp.bfloat16)
    branches = lax.psum_scatter(
        (
            jnp.dot(attended_all, out_full, preferred_element_type=jnp.float32)
            + jnp.dot(hidden_all, down_full, preferred_element_type=jnp.float32)
        ).astype(jnp.bfloat16),
        "mp",
        scatter_dimension=0,
        tiled=True,
    ).astype(jnp.float32)
    mixed = (inputs32 + branches + b_out + b_fc2).astype(jnp.bfloat16)
    grads_all = lax.all_gather(cotangent, "mp", axis=0, tiled=True)
    qkv_full, out_full, up_full, down_full = weights
    down_grad = jnp.einsum("gf,gd->fd", hidden_all, grads_all, preferred_element_type=jnp.float32)
    hidden_grad = jnp.einsum("gd,fd->gf", grads_all, down_full, preferred_element_type=jnp.float32)
    (pre_grad,) = gelu_back(hidden_grad)
    pre_low = pre_grad.astype(jnp.bfloat16)
    up_bias_grad = jnp.sum(pre_low, axis=0, dtype=jnp.float32)
    up_grad = jnp.einsum("gd,gf->df", normed_all, pre_low, preferred_element_type=jnp.float32)
    up_shard, down_shard = (
        summed_on_arrival(up_grad.astype(jnp.bfloat16), "dp", 0),
        summed_on_arrival(down_grad.astype(jnp.bfloat16), "dp", 1),
    )
    out_grad = jnp.einsum("ge,gd->ed", attended_all, grads_all, preferred_element_type=jnp.float32)
    attended_grad = jnp.einsum(
        "gd,ed->ge", grads_all, out_full, preferred_element_type=jnp.float32
    ).astype(jnp.bfloat16)
    grad_blocks = attended_grad.reshape(block_count, block_rows, local_heads, HD)

    def backward_block(carry, operands):
        key_acc, value_acc = carry
        query_blk, seg_blk, row_blk, log_blk, grad_blk = operands
        scores = masked_scores(query_blk, seg_blk, row_blk)
        probs = jnp.exp(scores - log_blk[..., None])
        probs_low = probs.astype(jnp.bfloat16)
        prob_grad = jnp.einsum(
            "qhd,khd->hqk", grad_blk, values_all, preferred_element_type=jnp.float32
        )
        centre = jnp.sum(probs * prob_grad, axis=-1, keepdims=True)
        score_grad = (probs * (prob_grad - centre)).astype(jnp.bfloat16)
        query_grad = (
            jnp.einsum("hqk,khd->qhd", score_grad, keys_all, preferred_element_type=jnp.float32)
            * scale
        )
        key_acc = (
            key_acc
            + jnp.einsum("hqk,qhd->khd", score_grad, query_blk, preferred_element_type=jnp.float32)
            * scale
        )
        value_acc = value_acc + jnp.einsum(
            "hqk,qhd->khd", probs_low, grad_blk, preferred_element_type=jnp.float32
        )
        return ((key_acc, value_acc), query_grad)

    zero_heads = jnp.zeros((group_rows, local_heads, HD), jnp.float32)
    (key_grad, value_grad), query_grads = lax.scan(
        backward_block,
        (zero_heads, zero_heads),
        (query_blocks, seg_blocks, row_blocks, log_totals, grad_blocks),
    )
    (query_pre,) = query_back(query_grads.reshape(group_rows, local_heads, HD))
    (key_pre,) = key_back(key_grad)
    qkv_grad = (
        jnp.stack([query_pre, key_pre, value_grad], axis=1)
        .reshape(group_rows, 3, local_width)
        .astype(jnp.bfloat16)
    )
    qkv_bias_grad = jnp.sum(qkv_grad, axis=0, dtype=jnp.float32)
    qkv_weight_grad = jnp.einsum(
        "gd,gte->dte", normed_all, qkv_grad, preferred_element_type=jnp.float32
    )
    from_qkv = jnp.einsum("gte,dte->gd", qkv_grad, qkv_full, preferred_element_type=jnp.float32)
    normed_grad = lax.psum_scatter(
        (
            from_qkv + jnp.einsum("gf,df->gd", pre_low, up_full, preferred_element_type=jnp.float32)
        ).astype(jnp.bfloat16),
        "mp",
        scatter_dimension=0,
        tiled=True,
    ).astype(jnp.float32)
    input_grad, gain_part, shift_part = norm_back(normed_grad)
    grads32 = cotangent.astype(jnp.float32)
    tokens_grad = (grads32 + input_grad).astype(jnp.bfloat16)
    qkv_shard, out_shard = (
        summed_on_arrival(qkv_weight_grad.astype(jnp.bfloat16), "dp", 0),
        summed_on_arrival(out_grad.astype(jnp.bfloat16), "dp", 1),
    )
    qkv_bias_sum, up_bias_sum = lax.psum((qkv_bias_grad, up_bias_grad), "dp")
    gain_sum, shift_sum, out_bias_sum = lax.psum(
        (gain_part, shift_part, jnp.sum(grads32, axis=0)), ("dp", "mp")
    )
    return (
        mixed,
        tokens_grad,
        qkv_shard,
        qkv_bias_sum,
        out_shard,
        out_bias_sum,
        up_shard,
        up_bias_sum,
        down_shard,
        out_bias_sum,
        gain_sum,
        shift_sum,
    )


def solution(mesh):
    in_specs = (
        P(("dp", "mp"), None),
        P(("dp", "mp"), None),
        P("dp", None),
        P("dp", None, "mp"),
        P(None, "mp"),
        P("mp", "dp"),
        P(),
        P("dp", "mp"),
        P("mp"),
        P("mp", "dp"),
        P(),
        P(),
        P(),
    )
    out_specs = (
        P(("dp", "mp"), None),
        P(("dp", "mp"), None),
        P("dp", None, "mp"),
        P(None, "mp"),
        P("mp", "dp"),
        P(),
        P("dp", "mp"),
        P("mp"),
        P("mp", "dp"),
        P(),
        P(),
        P(),
    )
    return jax.shard_map(
        per_device, mesh=mesh, in_specs=in_specs, out_specs=out_specs, check_vma=False
    )
```

profile of v0, /device:TPU:1, one launch (start us, length us, event | category | flops | bytes accessed | tf_op | source)
XLA Modules:
  0.0 679.9 jit_solution(11592091913506688907)
XLA Ops:
  18.2 36.9 %all-gather.9.cloned.1.call-done = bf16[2048,3,256]{0,2,1:T(8,128)(2,1)} async-done(((bf16[128,3,256]{0,2,1:T(8,128)(2,1)}), bf16[2048,3,256]{0,2,1:T(8,128)(2,1)}) %all-gather.9.cloned.1.call-update) | async-done | bytes 3145744 | tf_op jit(solution)/shard_map/all_gather | solution.py:84
  55.1 73.6 %all-gather.7.cloned.1.call-done = bf16[1024,2048]{1,0:T(8,128)(2,1)} async-done(((bf16[128,2048]{1,0:T(8,128)(2,1)}), bf16[1024,2048]{1,0:T(8,128)(2,1)}) %all-gather.7.cloned.1.call-update) | async-done | bytes 4194320 | tf_op jit(solution)/shard_map/all_gather | solution.py:90
  128.7 6.2 fusion.60
  136.5 26.7 %all-gather.11.cloned.1.call-done = bf16[256,2048]{1,0:T(8,128)(2,1)} async-done(((bf16[256,128]{1,0:T(8,128)(2,1)}), bf16[256,2048]{1,0:T(8,128)(2,1)}) %all-gather.11.cloned.1.call-update) | async-done | bytes 1048592 | tf_op jit(solution)/shard_map/all_gather | solution.py:85
  163.2 72.7 %all-gather.17.cloned.1.call-done = bf16[1024,2048]{1,0:T(8,128)(2,1)} async-done(((bf16[128,2048]{1,0:T(8,128)(2,1)}), bf16[1024,2048]{1,0:T(8,128)(2,1)}) %all-gather.17.cloned.1.call-update) | async-done | bytes 4194320 | tf_op jit(solution)/shard_map/all_gather | solution.py:145
  247.5 16.9 %while.28 = (s32[]{:T(128)}, bf16[2,512,256]{2,1,0:T(8,128)(2,1)}, f32[2,4,512]{2,1,0:T(4,128)S(1)}, s32[2,512]{1,0:T(2,128)S(1)}, s32[1024]{0:T(1024)S(1)}, /*i...) while((s32[]{:T(128)}, bf16[2,512,256]{2,1,0:T(8,128)(2,1)}, ...), condition=%wide.region_8.9_spmd.clone, body=%wide.region_5.8_spmd.clone.sunk | while | flops 563738624 | bytes 29966460 | solution.py:130
  264.4 50.4 %while.29 = (s32[]{:T(128)}, f32[1024,4,64]{0,2,1:T(8,128)S(1)}, f32[1024,4,64]{0,2,1:T(8,128)}, f32[2,512,4,64]{1,0,3,2:T(2,128)}, bf16[2,512,4,64]{1,3,2,0:T(8...) while((s32[]{:T(128)}, f32[1024,4,64]{0,2,1:T(8,128)S(1)}, ...), condition=%wide.region_12.13_spmd.clone, body=%wide.region_10.12_spmd.clone.sunk | while | flops 1376647168 | bytes 76619976 | solution.py:189
  278.6 10.4 %dynamic_update_slice.22 = f32[2,512,4,64]{1,0,3,2:T(2,128)} dynamic-update-slice(f32[2,512,4,64]{1,0,3,2:T(2,128)} %get-tuple-element.521, f32[1,512,4,64]{1,0,3,2:T(1,128)S(1)} %copy.123, s32[]{:T(128)S(6)} %copy.142, s32[]{:T(128)} %constant.45.clone.1..sunk, s32[]{:T(128)} %constant.45.clone.1..sunk, s32[]{:T(128)} %constant.45.clone.1..sunk) | dynamic-update-slice | bytes 1048580 | tf_op jit(solution)/shard_map/while/body/jit(dynamic_update_index_in_dim)/dynamic_update_slice | solution.py:189
  303.9 10.4 %dynamic_update_slice.22 = f32[2,512,4,64]{1,0,3,2:T(2,128)} dynamic-update-slice(f32[2,512,4,64]{1,0,3,2:T(2,128)} %get-tuple-element.521, f32[1,512,4,64]{1,0,3,2:T(1,128)S(1)} %copy.123, s32[]{:T(128)S(6)} %copy.142, s32[]{:T(128)} %constant.45.clone.1..sunk, s32[]{:T(128)} %constant.45.clone.1..sunk, s32[]{:T(128)} %constant.45.clone.1..sunk) | dynamic-update-slice | bytes 1048580 | tf_op jit(solution)/shard_map/while/body/jit(dynamic_update_index_in_dim)/dynamic_update_slice | solution.py:189
  319.6 10.0 %fusion.85 = f32[1024,1024]{1,0:T(8,128)} fusion(bf16[1024,2048]{1,0:T(8,128)(2,1)} %all-gather.7.cloned.1.call-done, bf16[2048,1024]{1,0:T(8,128)(2,1)} %all-gather.13.cloned.1.call-done), kind=kOutput, calls=%fused_computation.151 | convolution fusion | flops 4294967296 | bytes 12582912 | tf_op jit(solution)/shard_map/dot_general | solution.py:132
  329.7 11.7 %convert_reduce_fusion.3 = (f32[1024]{0:T(1024)S(1)}, bf16[1024,1024]{1,0:T(8,128)(2,1)S(1)}) fusion(f32[1024,1024]{1,0:T(8,128)} %fusion.85, f32[1024]{0:T(1024)S(1)} %copy-done.27, bf16[1024,2048]{1,0:T(8,128)(2,1)} %all-gather.17.cloned.1.call-done, bf16[1024,2048]{1,0:T(8,128)(2,1)} %all-gather.15.cloned.1.call-done), kind=kOutput, calls=%fused_computation.76 | convolution fusion | flops 4319083520 | bytes 14688256 | tf_op jit(solution)/shard_map/gd,fd->gf/dot_general | solution.py:148
  346.2 5.0 fusion.45
  356.9 5.6 all-to-all-start.1
  362.5 5.7 fusion.57
  370.3 9.9 %all-to-all-done.1 = bf16[16,256,128]{2,1,0:T(8,128)(2,1)S(1)} async-done(((bf16[16,256,128]{2,1,0:T(8,128)(2,1)}), bf16[16,256,128]{2,1,0:T(8,128)(2,1)S(1)}, u32[]{:S(2)}, u32[]{:S(2)}) %all-to-all-start.1) | async-done | bytes 1048608 | tf_op jit(solution)/shard_map/all_to_all | solution.py:17
  385.3 8.9 %convert_bitcast_fusion = bf16[128,16,8,128]{3,2,1,0:T(8,128)(2,1)S(1)} fusion(bf16[1024,2048]{1,0:T(8,128)(2,1)} %all-gather.17.cloned.1.call-done, f32[1024,1024]{1,0:T(8,128)} %fusion.85, f32[1024]{0:T(1024)S(1)} %copy-done.27), kind=kOutput, calls=%fused_computation.75 | convolution fusion | flops 4307550208 | bytes 12587008 | tf_op jit(solution)/shard_map/gf,gd->fd/dot_general | solution.py:147
  397.3 37.6 %all-to-all-done = bf16[16,128,3,256]{3,1,2,0:T(8,128)(2,1)S(1)} async-done(((bf16[16,128,3,256]{3,1,2,0:T(8,128)(2,1)}), bf16[16,128,3,256]{3,1,2,0:T(8,128)(2,1)S(1)}, u32[]{:S(2)}, u32[]{:S(2)}) %all-to-all-start) | async-done | bytes 3145760 | tf_op jit(solution)/shard_map/all_to_all | solution.py:17
  434.9 5.2 all-to-all-start.3
  440.2 8.8 %fusion.83 = f32[1024,2048]{1,0:T(8,128)S(1)} fusion(bf16[1024,2048]{1,0:T(8,128)(2,1)} %all-gather.15.cloned.1.call-done, f32[1024,1024]{1,0:T(8,128)} %fusion.85, f32[1024]{0:T(1024)S(1)} %copy-done.27), kind=kOutput, calls=%fused_computation.150 | convolution fusion | flops 4305453056 | bytes 16781312 | tf_op jit(solution)/shard_map/dot_general | solution.py:138
  452.3 9.4 %convolution_convert_fusion = bf16[2048,1024]{1,0:T(8,128)(2,1)} fusion(bf16[1024,2048]{1,0:T(8,128)(2,1)} %all-gather.7.cloned.1.call-done, bf16[1024,1024]{1,0:T(8,128)(2,1)} %copy-done.29), kind=kOutput, calls=%fused_computation.78 | convolution fusion | flops 4297064448 | bytes 10485760 | tf_op jit(solution)/shard_map/gd,gf->df/dot_general | solution.py:152
  461.7 39.2 %all-to-all-done.3 = bf16[16,1024,128]{2,1,0:T(8,128)(2,1)} async-done(((bf16[16,1024,128]{2,1,0:T(8,128)(2,1)}), bf16[16,1024,128]{2,1,0:T(8,128)(2,1)}, u32[]{:S(2)}, u32[]{:S(2)}) %all-to-all-start.3) | async-done | bytes 4194336 | tf_op jit(solution)/shard_map/all_to_all | solution.py:17
  500.9 5.3 all-to-all-start.2
  507.8 82.5 %all-reduce.7 = (f32[3,256]{1,0:T(4,128)}, f32[1024]{0:T(1024)}) all-reduce(f32[3,256]{1,0:T(4,128)S(1)} %convert_reduce_fusion.4, f32[1024]{0:T(1024)S(1)} %get-tuple-element.299), channel_id=1, replica_groups=mesh['dp'=16,'mp'=8] {'dp'}, use_global_device_ids=true, to_apply=%region_18.19 | all-reduce | flops 1792 | bytes 14336 | tf_op jit(solution)/shard_map/psum | solution.py:221
  607.3 64.7 %all-reduce.6 = (f32[2048]{0:T(1024)S(1)}, f32[2048]{0:T(1024)}, f32[2048]{0:T(1024)}) all-reduce(f32[2048]{0:T(1024)S(1)} %get-tuple-element.319, f32[2048]{0:T(1024)S(1)} %get-tuple-element.248, f32[2048]{0:T(1024)S(1)} %get-tuple-element.250), channel_id=1, replica_groups=mesh['dp'=16,'mp'=8] {'dp','mp'}, use_global_device_ids=true, to_apply=%region_21.22 | all-reduce | flops 6144 | bytes 49152 | tf_op jit(solution)/shard_map/psum | solution.py:222
  (179 shorter events, 117.4 us)
Async XLA Ops:
  7.2 10.3 %copy-start.28 = (s32[1,4]{1,0:T(1,128)S(1)}, s32[1,4]{1,0:T(1,128)}, u32[]{:S(2)}) copy-start(s32[1,4]{1,0:T(1,128)} %param.19) | copy-start | bytes 52
  7.2 121.5 %copy-start.26 = (f32[3,256]{1,0:T(4,128)S(1)}, f32[3,256]{1,0:T(4,128)}, u32[]{:S(2)}) copy-start(f32[3,256]{1,0:T(4,128)} %param.21) | copy-start | bytes 9220
  7.2 47.9 %all-gather.9.cloned.1.call-start = ((), (), s32[]{:S(2)}) async-start(), calls=%async_computation.7 | async-start | bytes 3342336 | tf_op jit(solution)/shard_map/all_gather | solution.py:84
  9.0 119.7 %all-gather.7.cloned.1.call-start = ((), (), s32[]{:S(2)}) async-start(), calls=%async_computation.6 | async-start | bytes 4718592 | tf_op jit(solution)/shard_map/all_gather | solution.py:90
  14.9 148.3 %all-gather.11.cloned.1.call-start = ((), (), s32[]{:S(2)}) async-start(), calls=%async_computation.8 | async-start | bytes 1114112 | tf_op jit(solution)/shard_map/all_gather | solution.py:85
  15.7 220.3 %all-gather.17.cloned.1.call-start = ((), (), s32[]{:S(2)}) async-start(), calls=%async_computation.12 | async-start | bytes 4718592 | tf_op jit(solution)/shard_map/all_gather | solution.py:145
  16.2 303.4 %all-gather.13.cloned.1.call-start = ((), (), s32[]{:S(2)}) async-start(), calls=%async_computation.9 | async-start | bytes 4456448 | tf_op jit(solution)/shard_map/all_gather | solution.py:86
  16.8 312.8 %all-gather.15.cloned.1.call-start = ((), (), s32[]{:S(2)}) async-start(), calls=%async_computation.10 | async-start | bytes 4456448 | tf_op jit(solution)/shard_map/all_gather | solution.py:87
  17.4 583.8 %reduce-scatter.5.cloned.1.call-start = ((), (), s32[]{:S(2)}) async-start(), calls=%async_computation.13 | async-start | bytes 4718592 | tf_op jit(solution)/shard_map/reduce_scatter | solution.py:206
  18.2 227.8 %copy-start.8 = (f32[1024,16]{0,1:T(8,128)}, f32[1024,16]{0,1:T(8,128)S(1)}, u32[]{:S(2)}) copy-start(f32[1024,16]{0,1:T(8,128)S(1)} %get-tuple-element.326) | copy-start | bytes 196612
  18.2 227.8 %copy-start.10 = (f32[1024,16]{0,1:T(8,128)}, f32[1024,16]{0,1:T(8,128)S(1)}, u32[]{:S(2)}) copy-start(f32[1024,16]{0,1:T(8,128)S(1)} %get-tuple-element.327) | copy-start | bytes 196612
  317.6 44.9 %copy-start.3 = (bf16[1024,1,256]{2,0,1:T(8,128)(2,1)}, bf16[1024,1,256]{2,0,1:T(8,128)(2,1)S(1)}, u32[]{:S(2)}) copy-start(bf16[1024,1,256]{2,0,1:T(8,128)(2,1)S(1)} %copy.73) | copy-start | bytes 1572868
  317.8 44.6 %copy-start.4 = (bf16[1024,1,256]{2,0,1:T(8,128)(2,1)}, bf16[1024,1,256]{2,0,1:T(8,128)(2,1)S(1)}, u32[]{:S(2)}) copy-start(bf16[1024,1,256]{2,0,1:T(8,128)(2,1)S(1)} %copy.72) | copy-start | bytes 1572868
  319.6 42.9 %copy-start.5 = (bf16[1024,1,256]{2,0,1:T(8,128)(2,1)}, bf16[1024,1,256]{2,0,1:T(8,128)(2,1)S(1)}, u32[]{:S(2)}) copy-start(bf16[1024,1,256]{2,0,1:T(8,128)(2,1)S(1)} %copy.74) | copy-start | bytes 1572868
  319.6 10.1 %copy-start.27 = (f32[1024]{0:T(1024)S(1)}, f32[1024]{0:T(1024)}, u32[]{:S(2)}) copy-start(f32[1024]{0:T(1024)} %param.25) | copy-start | bytes 12292
  329.7 11.7 %copy-start.24 = (bf16[2048,1024]{1,0:T(8,128)(2,1)S(1)}, bf16[2048,1024]{1,0:T(8,128)(2,1)}, u32[]{:S(2)}) copy-start(bf16[2048,1024]{1,0:T(8,128)(2,1)} %all-gather.13.cloned.1.call-done) | copy-start | bytes 12582916
  356.9 23.4 %all-to-all-start.1 = ((bf16[16,256,128]{2,1,0:T(8,128)(2,1)}), bf16[16,256,128]{2,1,0:T(8,128)(2,1)S(1)}, u32[]{:S(2)}, u32[]{:S(2)}) async-start(bf16[16,256,128]{2,1,0:T(8,128)(2,1)} %bitcast.127), calls=%async_computation.3 | async-start | bytes 2097152 | tf_op jit(solution)/shard_map/all_to_all | solution.py:17
  381.2 53.7 %all-to-all-start = ((bf16[16,128,3,256]{3,1,2,0:T(8,128)(2,1)}), bf16[16,128,3,256]{3,1,2,0:T(8,128)(2,1)S(1)}, u32[]{:S(2)}, u32[]{:S(2)}) async-start(bf16[16,128,3,256]{3,1,2,0:T(8,128)(2,1)} %copy.77), calls=%async_computation.2 | async-start | bytes 6291456 | tf_op jit(solution)/shard_map/all_to_all | solution.py:17
  434.9 66.0 %all-to-all-start.3 = ((bf16[16,1024,128]{2,1,0:T(8,128)(2,1)}), bf16[16,1024,128]{2,1,0:T(8,128)(2,1)}, u32[]{:S(2)}, u32[]{:S(2)}) async-start(bf16[16,1024,128]{2,1,0:T(8,128)(2,1)} %bitcast.172), calls=%async_computation.5 | async-start | bytes 8388608 | tf_op jit(solution)/shard_map/all_to_all | solution.py:17
  440.1 164.2 %reduce-scatter.3.cloned.1.call-start = ((), (), s32[]{:S(2)}) async-start(), calls=%async_computation.11 | async-start | bytes 4718592 | tf_op jit(solution)/shard_map/reduce_scatter | solution.py:135
  440.2 8.8 %copy-start.7 = (bf16[256,2048]{1,0:T(8,128)(2,1)S(1)}, bf16[256,2048]{1,0:T(8,128)(2,1)}, u32[]{:S(2)}) copy-start(bf16[256,2048]{1,0:T(8,128)(2,1)} %all-gather.11.cloned.1.call-done) | copy-start | bytes 3145732
  500.9 96.4 %all-to-all-start.2 = ((bf16[16,128,1024]{2,1,0:T(8,128)(2,1)}), bf16[16,128,1024]{2,1,0:T(8,128)(2,1)}, u32[]{:S(2)}, u32[]{:S(2)}) async-start(bf16[16,128,1024]{2,1,0:T(8,128)(2,1)} %bitcast.174), calls=%async_computation.4 | async-start | bytes 8388608 | tf_op jit(solution)/shard_map/all_to_all | solution.py:17
  593.6 9.1 %copy-start.23 = (f32[128]{0:T(128)S(1)}, f32[128]{0:T(128)}, u32[]{:S(2)}) copy-start(f32[128]{0:T(128)} %copy-done.22) | copy-start | bytes 1540
  593.6 9.1 %copy-start.21 = (f32[128]{0:T(128)S(1)}, f32[128]{0:T(128)}, u32[]{:S(2)}) copy-start(f32[128]{0:T(128)} %copy-done.20) | copy-start | bytes 1540
  (19 other events, 75.6 us)
Sparse Core Ops, SparseCore 0:
  10.2 44.8 all-gather.8
  58.0 70.6 all-gather.6
  130.3 32.7 all-gather.10
  165.4 70.4 all-gather.16
  237.5 36.1 all-gather.12
  275.1 45.2 all-gather.14
  351.3 99.5 reduce-scatter.4
  455.2 108.9 reduce-scatter.2
where the time goes:
time: 690 us; the launch traced here: 680 us
  waiting for transfers between devices  299 us (43%)
  blocking collectives  147 us (21%)
  matrix products  113 us (16%)
  local copies, waits for them, and re-layouts  45.5 us (7%)
  other arithmetic  38.9 us (6%)
  starting transfers between devices  20.5 us (3%)
  between operations  15.2 us (2%)
    all_to_all x4, waiting for transfers between devices, summed_on_arrival(): lax.all_to_all(tiles, axis, split_axis=0, concat_axis=0, tiled=True)  86.8 us
    psum x1, blocking collectives, per_device(): qkv_bias_sum, up_bias_sum = lax.psum((qkv_bias_grad, up_bias_grad), 'dp')  82.5 us
    all_gather x1, waiting for transfers between devices, per_device(): lax.all_gather(normed.astype(jnp.bfloat16), 'mp', axis=0, tiled=True)  73.6 us
    all_gather x1, waiting for transfers between devices, per_device(): grads_all = lax.all_gather(cotangent, 'mp', axis=0, tiled=True)  72.7 us
    psum x1, blocking collectives, per_device(): lax.psum((gain_part, shift_part, jnp.sum(grads32, axis=0)), ('dp', 'mp'))  64.7 us
    all_gather x1, waiting for transfers between devices, per_device(): lax.all_gather(w_qkv, 'dp', axis=0, tiled=True)  36.9 us
    all_gather x1, waiting for transfers between devices, per_device(): lax.all_gather(w_out, 'dp', axis=1, tiled=True)  26.7 us
    dynamic_update_slice x4, local copies, waits for them, and re-layouts, per_device(): lax.scan(backward_block, (zero_heads, zero_heads), (query_blocks, seg_blo...  21.9 us
  transfers between devices with their start and end apart: 12, of which 7 were waited for; matrix products, arithmetic and copies ran while one was open for 25% of the time, Pallas kernels for 0%

commit v1 on v0

v1 whole, which is shorter than its diff:
```python
import jax
import jax.numpy as jnp
import numpy as np
from jax import lax
from jax.experimental import pallas as pl
from jax.experimental.pallas import tpu as pltpu
from jax.sharding import PartitionSpec as P

HD = 64
ROT = 32
MESH = pl.DeviceIdType.MESH
BF16 = jnp.bfloat16
F32 = jnp.float32
ROWS = 128
GROUP = 1024
D = 2048
QKV = 768
FC = 1024
IN_W = QKV + FC
OUT_W = 256 + FC
ALL_W = IN_W + OUT_W
LOG2E = 1.4426950408889634
LN2 = 0.6931471805599453
CHUNKS = 4
CHUNK = D // CHUNKS
KEEP = 96
VMEM_LIMIT = 64 * 1024 * 1024 - 65536

ORDER = (
    "Wi.go", "ln", "X.go", "X.x", "wprep", "tab", "Wi.f1", "X.f1", "Wi.p", "Wi.c1", "Y.x", "X.p", "X.q1", "X.q2",
    "Wi.f2", "Wi.c2", "Wo.go", "Wo.x", "X.f2", "Y.go", "Wi.c3", "Wo.f1", "proj", "Y.f1", "Y.q1", "Y.p", "Wo.p",
    "Wo.c1", "attf", "Wo.f2", "Wo.c2", "Y.q2", "Wo.c3", "Y.f2", "p1", "r10_qa", "backs", "r10_s1b", "r11_qa",
    "r11_s1b", "r12_qa", "r13_qa", "dwo0", "r10_s1a", "dwo1", "dwo2", "ko.t0", "dwo3", "ko.t1", "attb0", "r10_th",
    "r11_s1a", "r12_s1a", "r12_s1b", "ko.t2", "ko.t3", "ro.s1b", "attb1", "r11_th", "r12_th", "r13_s1a", "r13_s1b",
    "ro.s1a", "bias", "p2.0", "p2.1", "r13_th", "p2.2", "r20_s1b", "ro.th", "p2.3", "r20_qa", "r21_s1b", "pool",
    "dwi0", "dwi1", "mix", "r20_s1a", "r21_qa", "kq.t0", "dwi2", "r22_qa", "kf.t0", "kf.t1", "r23_qa", "kq.t1",
    "dwi3", "kq.t2", "kf.t2", "rq.s1b", "rq.s1a", "r20_th", "r22_s1b", "r21_s1a", "kq.t3", "kf.t3", "r22_s1a",
    "r21_th", "r23_s1a", "r23_s1b", "r22_th", "rf.s1b", "r23_th", "rf.s1a", "sums", "rq.th", "lasto", "back",
    "sum_x", "sum_z", "lastq", "rf.th", "sum_y", "lastf",
)

VMEM = pl.BlockSpec(memory_space=pltpu.VMEM)
ANY = pl.BlockSpec(memory_space=pl.ANY)


def place():
    dp = lax.axis_index("dp")
    mp = lax.axis_index("mp")
    return dp, mp


def peers():
    dp, mp = place()
    z, low = dp // 4, dp % 4
    y, xh = mp // 2, mp % 2
    core = low % 2
    xl = low // 2
    flipped = z * 4 + (1 - xl) * 2 + core
    return {
        "core": (z * 4 + xl * 2 + (1 - core), mp),
        "xp": (flipped, y * 2 + (xh + xl) % 2),
        "xm": (flipped, y * 2 + (xh + 1 - xl) % 2),
        "xx": (dp, y * 2 + (1 - xh)),
        "xl": (flipped, mp),
        "xp2": (flipped + 1 - 2 * core, y * 2 + (xh + xl) % 2),
        "xm2": (flipped + 1 - 2 * core, y * 2 + (xh + 1 - xl) % 2),
        "xx2": (dp + 1 - 2 * core, y * 2 + (1 - xh)),
        "zp": (((z + 1) % 4) * 4 + low, mp),
        "zm": (((z + 3) % 4) * 4 + low, mp),
        "zz": (((z + 2) % 4) * 4 + low, mp),
        "yp": (dp, ((y + 1) % 4) * 2 + xh),
        "ym": (dp, ((y + 3) % 4) * 2 + xh),
        "yy": (dp, ((y + 2) % 4) * 2 + xh),
    }


class remote:
    def __init__(self, src, dst, send, recv, target):
        self.parts = dict(
            src_ref=src, dst_ref=dst, send_sem=send, recv_sem=recv, device_id=target, device_id_type=MESH
        )

    def start(self):
        pltpu.make_async_remote_copy(**self.parts).start()

    def wait(self):
        pltpu.make_async_remote_copy(**self.parts).wait()

    def wait_send(self):
        pltpu.make_async_remote_copy(**self.parts).wait_send()

    def wait_recv(self):
        pltpu.make_async_remote_copy(**self.parts).wait_recv()


def rows_at(start, count):
    return pl.ds(pl.multiple_of(start, 16), count)


def mp_slots():
    _, mp = place()
    y, xh = mp // 2, mp % 2

    def at(step):
        base = ((y + step) % 4) * 2
        return (base + xh, base + (1 - xh))

    return mp, at(0)[1], at(1), at(3), at(2)


def dp_slots():
    dp, _ = place()
    z, xl, core = dp // 4, (dp // 2) % 2, dp % 2

    def at(step):
        base = ((z + step) % 4) * 4 + core
        return (base + xl * 2, base + (1 - xl) * 2)

    return dp, at(0)[1], at(1), at(3), at(2)


class RingGather:
    def __init__(self, piece, slots, pair, up, down, send, recv, keep=ROWS):
        slot, pair_slot, plus, minus, opposite = slots
        half, mid = ROWS // 2, keep // 2

        def copy(index, which, target, start=0, count=ROWS):
            part = piece(which, start, count)
            return remote(part, part, send.at[index], recv.at[index], target)

        self.go = [
            copy(0, slot, pair),
            copy(1, slot, up),
            copy(2, slot, down),
            copy(3, pair_slot, up, 0, keep),
            copy(4, pair_slot, down, 0, keep),
            copy(5, minus[0], up, 0, half),
            copy(6, plus[0], down, half, half),
            copy(7, minus[1], up, 0, mid),
            copy(8, plus[1], down, mid, mid),
        ]
        self.come = [
            copy(0, pair_slot, pair),
            copy(1, minus[0], up),
            copy(2, plus[0], down),
            copy(3, minus[1], up, 0, keep),
            copy(4, plus[1], down, 0, keep),
            copy(5, opposite[0], up, 0, half),
            copy(6, opposite[0], down, half, half),
            copy(7, opposite[1], up, 0, mid),
            copy(8, opposite[1], down, mid, mid),
        ]
        if keep < ROWS:
            for index, two in ((9, minus), (10, plus), (11, opposite)):
                self.go.append(copy(index, two[0], pair, keep, ROWS - keep))
                self.come.append(copy(index, two[1], pair, keep, ROWS - keep))

    def start(self, *which):
        for i in which:
            self.go[i].start()

    def arrived(self, *which):
        for i in which:
            self.come[i].wait_recv()

    def sent(self):
        for c in self.go:
            c.wait_send()


class CoreShare:
    def __init__(self, ref, target, send, recv):
        slot, pair_slot, plus, minus, opposite = dp_slots()
        half = ROWS // 2
        flip = 1 - 2 * (place()[0] % 2)
        pieces = [
            (pair_slot, 0, ROWS),
            (minus[0], 0, ROWS),
            (plus[0], 0, ROWS),
            (minus[1], 0, ROWS),
            (plus[1], 0, ROWS),
            (opposite[0], 0, half),
            (opposite[0], half, half),
            (opposite[1], 0, half),
            (opposite[1], half, half),
            (slot, 0, ROWS),
        ]

        def copy(index, which, start, count):
            piece = ref.at[rows_at(which * ROWS + start, count)]
            return remote(piece, piece, send.at[index], recv.at[index], target)

        self.go = [copy(i, s, a, n) for i, (s, a, n) in enumerate(pieces)]
        self.come = [copy(i, s + flip, a, n) for i, (s, a, n) in enumerate(pieces)]

    def start(self, *which):
        for i in which:
            self.go[i].start()

    def arrived(self):
        for c in self.come:
            c.wait_recv()

    def sent(self):
        for c in self.go:
            c.wait_send()


def each(count, body, size=16, start=0):
    def step(i, carry):
        body(pl.ds(pl.multiple_of(i * size, size), size))
        return carry

    lax.fori_loop(start // size, count // size, step, 0)


def add_into(dst, term):
    def body(at):
        dst[at, :] = dst[at, :] + term[at, :]

    each(dst.shape[0], body, 32)


class RingReduce:
    def __init__(self, part, slots, who, names, half, full, across, send, recv, keep=ROWS, rest=()):
        slot, pair_slot, plus, minus, opposite = slots
        pair, up, down = (who[name] for name in names)
        self.part, self.slot, self.full, self.across = part, slot, full, across
        self.half, self.keep = half, keep
        self.pair_part = part(pair_slot, keep)
        self.plus_own, self.minus_pair = part(plus[0], ROWS), part(minus[1], keep)

        def go(index, src, dst, target):
            return remote(src, dst, send.at[index], recv.at[index], target)

        self.sends = [
            go(0, part(opposite[0], ROWS), half(0, ROWS), up),
            go(1, part(opposite[1], keep), half(1, keep), down),
            go(2, part(plus[1], keep), full(0, 1, keep), up),
            go(3, part(minus[0], ROWS), full(1, 0, ROWS), down),
            go(4, self.plus_own, full(0, 0, ROWS), up),
            go(5, self.minus_pair, full(1, 1, keep), down),
            go(6, self.pair_part, across, pair),
        ]
        if rest:
            rest_of, self.rest, self.rest_at = rest
            self.sends.append(go(7, rest_of, self.rest, pair))

    def start(self, *which):
        for i in which:
            self.sends[i].start()

    def add_rest(self):
        self.sends[7].wait_recv()
        for place_on_ring in range(4):
            add_into(self.rest_at(place_on_ring), self.rest.at[place_on_ring])

    def up_term(self):
        self.sends[0].wait_recv()
        add_into(self.plus_own, self.half(0, ROWS))
        self.start(4)

    def down_term(self):
        self.sends[1].wait_recv()
        add_into(self.minus_pair, self.half(1, self.keep))
        self.start(5)

    def third(self):
        for i in (2, 3, 4, 5):
            self.sends[i].wait_recv()
        dst, a, b = self.pair_part, self.full(0, 1, self.keep), self.full(1, 1, self.keep)

        def body(at):
            total = dst[at, :].astype(F32) + a[at, :].astype(F32) + b[at, :].astype(F32)
            dst[at, :] = total.astype(dst.dtype)

        each(self.keep, body, 32)
        self.start(6)

    def arrived(self):
        self.sends[6].wait_recv()

    def total(self, at):
        return (
            self.part(self.slot, ROWS)[at, :].astype(F32)
            + self.full(0, 0, ROWS)[at, :].astype(F32)
            + self.full(1, 0, ROWS)[at, :].astype(F32)
            + self.across[at, :].astype(F32)
        )

    def sent(self):
        for c in self.sends:
            c.wait_send()


def dot_nn(a, b):
    return jnp.dot(a, b, preferred_element_type=F32)


def dot_nt(a, b):
    return lax.dot_general(a, b, (((1,), (1,)), ((), ())), preferred_element_type=F32)


def dot_tn(a, b):
    return lax.dot_general(a, b, (((0,), (0,)), ((), ())), preferred_element_type=F32)


def block_kernel(
    tokens_in, cot_in, lens, wq, bq, wo_in, bo, wf1, b1, wf2_in, b2, gain, shift, freq, sign,
    mixed_out, tgrad_out, gin_out, gout_out, small_out,
    tokens, cot, wo, wf2, gin, gout, small, into, out_of,
    x, y, win, wout, ah, qp, dout, pool, p1, cos, sin, dk, dv,
    h1, f1, a1, q1, h2, f2, a2, q2, hi, fi, ai, ho, fo, ao, co, got_x, got, kt, vt,
    xs, xr, ys, yr, wis, wir, cis, cir, wos, wor, cos_s, cos_r,
    r1s, r1r, r2s, r2r, rfs, rfr, rqs, rqr, ros, ror, kfs, kfr, kqs, kqr, kos, kor, sms, smr, free,
):
    who = peers()
    dp, mp = place()
    core, xl, xh = dp % 2, (dp // 2) % 2, mp % 2
    z, yy = dp // 4, mp // 2
    barrier = pltpu.get_barrier_semaphore()
    met = [who[n] for n in ("core", "xp", "xm", "xx", "xp2", "xm2", "xx2", "zp", "zm", "zz", "yp", "ym", "yy")]
    for target in met:
        pl.semaphore_signal(barrier, inc=1, device_id=target, device_id_type=MESH)

    wrow = rows_at(dp * ROWS, ROWS)
    brought = [(wq.at[t], win.at[wrow, t * 256 : (t + 1) * 256]) for t in range(3)]
    brought += [(wf1, win.at[wrow, QKV:IN_W]), (tokens_in, tokens), (wo_in, wo), (wf2_in, wf2)]
    brought += [(cot_in, cot), (cot_in, y.at[yy, xh])]
    brought = [pltpu.make_async_copy(src, dst, into.at[i]) for i, (src, dst) in enumerate(brought)]
    for c in brought:
        c.start()

    def bring(*which):
        for i in which:
            brought[i].wait()

    def send_out(index, src, dst):
        pltpu.make_async_copy(src, dst, out_of.at[index]).start()

    mixed, tgrad = p1.at[yy, xh], y.at[yy, xh]
    outputs = ((mixed, mixed_out), (tgrad, tgrad_out), (gin, gin_out), (gout, gout_out), (small, small_out))
    pl.semaphore_wait(barrier, len(met))

    def flat(ref):
        return lambda slot, start, count: ref.at[rows_at(slot * ROWS + start, count)]

    def deep(ref):
        return lambda slot, start, count: ref.at[slot // 2, slot % 2, start : start + count]

    gx = RingGather(flat(x), mp_slots(), who["xx"], who["yp"], who["ym"], xs, xr, KEEP)
    gy = RingGather(deep(y), mp_slots(), who["xx"], who["yp"], who["ym"], ys, yr, KEEP)
    gi = RingGather(flat(win), dp_slots(), who["xl"], who["zp"], who["zm"], wis, wir)
    go = RingGather(flat(wout), dp_slots(), who["xl"], who["zp"], who["zm"], wos, wor)
    ci = CoreShare(win, who["core"], cis, cir)
    co_ = CoreShare(wout, who["core"], cos_s, cos_r)
    steps = {}

    def step(function):
        steps[function.__name__] = function
        return function

    def transfers(name, *actions):
        def act():
            for action, *which in actions:
                action(*which)

        steps[name] = act

    transfers("Wi.go", (bring, 0, 1, 2, 3), (gi.start, 1, 2, 0), (ci.start, 9))
    transfers("Wi.p", (gi.arrived, 0), (gi.start, 3, 4))
    transfers("Wi.f1", (gi.arrived, 1), (gi.start, 5), (gi.arrived, 2), (gi.start, 6))
    transfers("Wi.f2", (gi.arrived, 3), (gi.start, 7), (gi.arrived, 4), (gi.start, 8))
    transfers("Wi.c1", (ci.start, 0, 1, 2))
    transfers("Wi.c2", (ci.start, 3, 4))
    transfers("Wi.c3", (gi.arrived, 5, 6, 7, 8), (ci.start, 5, 6, 7, 8))
    transfers("Wo.go", (go.start, 1, 2), (co_.start, 9))
    transfers("Wo.x", (go.start, 0))
    transfers("Wo.p", (go.arrived, 0), (go.start, 3, 4))
    transfers("Wo.f1", (go.arrived, 1), (go.start, 5), (go.arrived, 2), (go.start, 6))
    transfers("Wo.f2", (go.arrived, 3), (go.start, 7), (go.arrived, 4), (go.start, 8))
    transfers("Wo.c1", (co_.start, 0, 1, 2))
    transfers("Wo.c2", (co_.start, 3, 4))
    transfers("Wo.c3", (go.arrived, 5, 6, 7, 8), (co_.start, 5, 6, 7, 8))
    for name, ring in (("X", gx), ("Y", gy)):
        transfers(f"{name}.p", (ring.arrived, 0), (ring.start, 3, 4))
        transfers(f"{name}.f1", (ring.arrived, 1), (ring.start, 5), (ring.arrived, 2), (ring.start, 6))
        transfers(f"{name}.f2", (ring.arrived, 3), (ring.start, 7), (ring.arrived, 4), (ring.start, 8))
        transfers(f"{name}.q1", (ring.start, 9, 10))
        transfers(f"{name}.q2", (ring.arrived, 6), (ring.start, 11))
    transfers("X.go", (gx.start, 1, 2))
    transfers("X.x", (gx.start, 0))
    transfers("Y.go", (gy.start, 1, 2))
    transfers("Y.x", (gy.start, 0))

    def norm_rows(i, carry):
        at = pl.ds(pl.multiple_of(i * 16, 16), 16)
        values = tokens[at, :].astype(F32)
        center = values - jnp.mean(values, axis=-1, keepdims=True)
        spread = jnp.mean(center * center, axis=-1, keepdims=True)
        normed = center * lax.rsqrt(spread + 1e-05) * gain[...] + shift[...]
        x[rows_at(mp * ROWS + i * 16, 16), :] = normed.astype(BF16)
        return carry

    @step
    def ln():
        bring(4)
        lax.fori_loop(0, ROWS // 16, norm_rows, 0)

    @step
    def wprep():
        bring(5, 6, 7, 8)
        wout[wrow, 0:256] = wo[...].astype(F32).T.astype(BF16)
        for j in range(8):
            part = wf2[j * 128 : (j + 1) * 128, :].astype(F32).T.astype(BF16)
            wout[wrow, 256 + j * 128 : 256 + (j + 1) * 128] = part

    def begin_of(row):
        e0 = lens[0, 0]
        e1 = e0 + lens[0, 1]
        e2 = e1 + lens[0, 2]
        first = jnp.where(row >= e0, e0, 0)
        return jnp.where(row >= e2, e2, jnp.where(row >= e1, e1, first))

    def tables(i, carry):
        at = rows_at(i * 64, 64)
        row = lax.broadcasted_iota(jnp.int32, (64, 1), 0) + i * 64
        angle = (row - begin_of(row)).astype(F32) * freq[...]
        cos[at, :] = jnp.cos(angle)
        sin[at, :] = jnp.sin(angle) * sign[...]
        return carry

    @step
    def tab():
        lax.fori_loop(0, GROUP // 64, tables, 0)

    lanes = lax.broadcasted_iota(jnp.int32, (1, 128), 1)
    head_mask = (lanes < HD, lanes >= HD)
    first_half = lanes % ROT < ROT // 2

    def turn(values, at, way):
        swapped = jnp.where(first_half, pltpu.roll(values, 112, 1), pltpu.roll(values, 16, 1))
        return values * cos[at, :] + swapped * (sin[at, :] * way)

    def project(half):
        at = rows_at(half * 512, 512)
        xb = x[at, :]
        products = dot_nn(xb, win[:, 0:QKV])
        for t in range(3):
            pre = products[:, t * 256 : (t + 1) * 256] + bq[t : t + 1, :]
            for j in range(2):
                part = pre[:, j * 128 : (j + 1) * 128]
                if t < 2:
                    part = turn(part, at, 1.0)
                if t == 0:
                    part = part * (HD**-0.5 * LOG2E)
                qp[at, t * 256 + j * 128 : t * 256 + (j + 1) * 128] = part.astype(BF16)

        def hidden(j, carry):
            cols = pl.ds(pl.multiple_of(j * 512, 256), 512)
            wcols = pl.ds(pl.multiple_of(QKV + j * 512, 256), 512)
            pre = dot_nn(x[at, :], win[:, wcols]) + b1[:, cols]
            square = pre * pre
            slope = 0.7978845608028654 * (1.0 + 0.134145 * square)
            t = jnp.tanh(0.7978845608028654 * pre * (1.0 + 0.044715 * square))
            half_up = 0.5 * (1.0 + t)
            ah[at, pl.ds(pl.multiple_of(256 + j * 512, 256), 512)] = (pre * half_up).astype(BF16)
            qp[at, wcols] = (half_up + 0.5 * pre * (1.0 - t * t) * slope).astype(BF16)
            return carry

        lax.fori_loop(0, FC // 512, hidden, 0)

    @step
    def proj():
        ci.arrived()
        gx.arrived(5, 7, 8, 9, 10, 11)

        def part(i, carry):
            project(i)
            return carry

        lax.fori_loop(0, 2, part, 0)

    stack = {7: (0, 0), 6: (0, 8), 2: (0, 15), 5: (1, 0), 4: (1, 6), 3: (1, 11), 1: (1, 15), 0: (1, 17)}

    def both(part):
        none = jnp.zeros_like(part)
        return jnp.concatenate([jnp.where(mask, part, none) for mask in head_mask], axis=0)

    def own_parts(product):
        return jnp.concatenate([product[0:HD, 0:128], product[HD:128, 128:256]], axis=0).T

    def kept(pair, i):
        side, row = stack[i]
        cols = pl.ds(pl.multiple_of(pair * 512 + side * 256, 256), 256)
        return pool.at[row * 128 : (row + i + 1) * 128, cols]

    def attend(pair, carry):
        qcols = pl.ds(pl.multiple_of(pair * 128, 128), 128)
        kcols = pl.ds(pl.multiple_of(256 + pair * 128, 128), 128)
        vcols = pl.ds(pl.multiple_of(512 + pair * 128, 128), 128)
        for i in range(4):
            at = pl.ds(i * 256, 256)
            kt[qcols, at] = qp[at, kcols].astype(F32).T.astype(BF16)
            vt[qcols, at] = qp[at, vcols].astype(F32).T.astype(BF16)
        for i in range(8):
            at = pl.ds(i * 128, 128)
            deep = (i + 1) * 128
            key_row = lax.broadcasted_iota(jnp.int32, (deep, 256), 0)
            row = (lax.broadcasted_iota(jnp.int32, (1, 256), 1) & 127) + i * 128
            allowed = (key_row >= begin_of(row)) & (key_row <= row)
            s = jnp.where(allowed, dot_nt(qp[:deep, kcols], both(qp[at, qcols])), -1e30)
            ex = jnp.exp2(s - jnp.max(s, axis=0, keepdims=True))
            probs = (ex * (1.0 / jnp.sum(ex, axis=0, keepdims=True))).astype(BF16)
            kept(pair, i)[...] = probs
            ah[at, qcols] = own_parts(dot_nn(vt[qcols, :deep], probs)).astype(BF16)
        return carry

    transfers("attf", (lax.fori_loop, 0, 2, attend, 0))

    def chunk(src, h, f, a, q, send, recv, c):
        cols = pl.ds(pl.multiple_of(c * CHUNK, CHUNK), CHUNK)
        return RingReduce(
            lambda slot, count: src.at[slot // 2, slot % 2, 0:count, cols],
            mp_slots(),
            who,
            ("xx", "yp", "ym"),
            lambda i, count: h.at[i, 0:count, cols],
            lambda i, j, count: f.at[i, j, 0:count, cols],
            a.at[:, cols],
            send.at[c],
            recv.at[c],
            KEEP,
            (
                src.at[:, 1 - xh, KEEP:ROWS, cols],
                q.at[:, :, cols],
                lambda place_on_ring: src.at[place_on_ring, xh, KEEP:ROWS, cols],
            ),
        )

    def r1(c):
        return chunk(p1, h1, f1, a1, q1, r1s, r1r, c)

    def r2(c):
        return chunk(y, h2, f2, a2, q2, r2s, r2r, c)

    def over_dp(src, h, f, a, send, recv, cols):
        return RingReduce(
            lambda slot, count: src.at[rows_at(slot * ROWS, count), cols],
            dp_slots(),
            who,
            ("xl", "zp", "zm"),
            lambda i, count: h.at[i, 0:count, cols],
            lambda i, j, count: f.at[i, j, 0:count, cols],
            a.at[:, cols],
            send,
            recv,
        )

    out_cols, fc_cols, qkv_cols = pl.ds(0, OUT_W), pl.ds(QKV, FC), pl.ds(0, QKV)
    ro = over_dp(wout, ho, fo, ao, ros, ror, out_cols)
    rf = over_dp(win, hi, fi, ai, rfs, rfr, fc_cols)
    rq = over_dp(win, hi, fi, ai, rqs, rqr, qkv_cols)

    def total(src, f, a, at, with_pair):
        terms = [src[yy, xh, at, :], f[0, 0, at, :], f[1, 0, at, :]]
        if with_pair:
            terms.append(a[at, :])
        terms = [term.astype(F32) for term in terms]
        return sum(terms[1:], terms[0])

    def each_row_block(body):
        each(KEEP, lambda at: body(at, True))
        each(ROWS, lambda at: body(at, False), start=KEEP)

    def spread_columns(src, w, dst, reduced, c):
        cols = pl.ds(pl.multiple_of(c * CHUNK, CHUNK), CHUNK)

        def part(i, carry):
            at = rows_at(i * 512, 512)
            product = dot_nt(src[at, :], w[cols, :]).astype(BF16)
            dst[pl.ds(i * 2, 2), :, :, cols] = product.reshape(2, 2, ROWS, CHUNK)
            return carry

        lax.fori_loop(0, GROUP // 512, part, 0)
        reduced(c).start(7, 1, 2)

    def branches(c, carry):
        spread_columns(ah, wout, p1, r1, c)
        return carry

    transfers("p1", (co_.arrived,), (lax.fori_loop, 0, CHUNKS, branches, 0))

    def back_rows(i):
        at = rows_at(i * 512, 512)
        dout[at, :] = dot_nn(y[pl.ds(i * 2, 2)].reshape(512, D), wout[:, 0:256]).astype(BF16)

        def hidden(j, carry):
            wcols = pl.ds(pl.multiple_of(256 + j * 512, 256), 512)
            cols = pl.ds(pl.multiple_of(QKV + j * 512, 256), 512)
            grad = dot_nn(y[pl.ds(i * 2, 2)].reshape(512, D), wout[:, wcols])
            qp[at, cols] = (grad * qp[at, cols].astype(F32)).astype(BF16)
            return carry

        lax.fori_loop(0, FC // 512, hidden, 0)

    @step
    def backs():
        gy.arrived(5, 7, 8, 9, 10, 11)

        def part(i, carry):
            back_rows(i)
            return carry

        lax.fori_loop(0, 2, part, 0)
        for item in (gi, go, ci, co_, gy, gx):
            item.sent()

    def crossing(dst, landing_of, cols, send, recv):
        copies, takes = [], []
        for n, step in enumerate((2, 1, 3, 0)):
            for two in range(2):
                slot = ((z + step) % 4) * 4 + two * 2 + core
                other = slot + 1 - 2 * core
                i = 2 * n + two
                landing = landing_of(i)
                copies.append(
                    remote(dst.at[rows_at(other * ROWS, ROWS), cols], landing, send.at[i], recv.at[i], who["core"])
                )
                takes.append((dst.at[rows_at(slot * ROWS, ROWS), cols], landing))
        return copies, takes

    def landing_out(i):
        return co.at[rows_at(i * ROWS, ROWS)]

    def landing_fc(i):
        return pool.at[rows_at(i * ROWS, ROWS)]

    def landing_qkv(i):
        return pool.at[rows_at(GROUP + i * ROWS, ROWS), 0:QKV]

    out_copies, out_takes = crossing(wout, landing_out, out_cols, kos, kor)
    fc_copies, fc_takes = crossing(win, landing_fc, fc_cols, kfs, kfr)
    qkv_copies, qkv_takes = crossing(win, landing_qkv, qkv_cols, kqs, kqr)

    def take(copies, takes, *which):
        for i in which:
            copies[i].wait_recv()
            add_into(*takes[i])

    def weight_grad(act, grad, dst, n, *copies):
        base = ((z + (2, 1, 3, 0)[n]) % 4) * 512

        def part(two, carry):
            cols = pl.ds(pl.multiple_of(base + two * 256, 256), 256)
            dst[cols, :] = dot_tn(act(cols), grad[...]).astype(BF16)
            return carry

        lax.fori_loop(0, 2, part, 0)
        for some in copies:
            some[2 * n].start()
            some[2 * n + 1].start()

    def x_cols(cols):
        return x[:, cols]

    def y_cols(cols):
        return y[:, :, :, cols].reshape(GROUP, 256)

    for n in range(4):
        transfers(f"dwo{n}", (weight_grad, y_cols, ah, wout, n, out_copies))
        transfers(f"dwi{n}", (weight_grad, x_cols, qp, win, n, fc_copies, qkv_copies))
    for name, copies, takes, ring in (
        ("ko", out_copies, out_takes, ro),
        ("kf", fc_copies, fc_takes, rf),
        ("kq", qkv_copies, qkv_takes, rq),
    ):
        for n, go_on in enumerate(((0, 1), (2,), (3,), ())):
            transfers(f"{name}.t{n}", (take, copies, takes, 2 * n, 2 * n + 1), (ring.start, *go_on))
    for name, ring in (("ro", ro), ("rf", rf), ("rq", rq)):
        transfers(f"{name}.s1a", (ring.up_term,))
        transfers(f"{name}.s1b", (ring.down_term,))
        transfers(f"{name}.th", (ring.third,))
    for name, ring in (("r1", r1), ("r2", r2)):
        for c in range(CHUNKS):
            part = ring(c)
            transfers(f"{name}{c}_qa", (part.add_rest,), (part.start, 0, 3))
            transfers(f"{name}{c}_s1a", (part.up_term,))
            transfers(f"{name}{c}_s1b", (part.down_term,))
            transfers(f"{name}{c}_th", (part.third,))

    def attend_back(pair):
        qcols = pl.ds(pair * 128, 128)
        kcols = pl.ds(256 + pair * 128, 128)
        vcols = pl.ds(512 + pair * 128, 128)
        dk[...] = jnp.zeros_like(dk)
        dv[...] = jnp.zeros_like(dv)
        for i in range(8):
            at = pl.ds(i * 128, 128)
            deep = (i + 1) * 128
            do2 = dout[at, qcols]
            queries, grads = both(qp[at, qcols]), both(do2)
            prod = (do2.astype(F32) * ah[at, qcols].astype(F32)).T
            centre = jnp.concatenate(
                [jnp.sum(prod[h * HD : (h + 1) * HD], axis=0, keepdims=True) for h in range(2)], axis=1
            )
            probs = kept(pair, i)[...]
            ds = (probs.astype(F32) * (dot_nt(qp[:deep, vcols], grads) - centre)).astype(BF16)
            dq = own_parts(dot_nn(kt[qcols, :deep], ds)) * (HD**-0.5)
            dk[:deep, :] += dot_nn(ds, queries)
            dv[:deep, :] += dot_nn(probs, grads)
            qp[at, qcols] = turn(dq, at, -1.0).astype(BF16)
        for i in range(4):
            at = pl.ds(i * 256, 256)
            qp[at, kcols] = turn(dk[at, :] * LN2, at, -1.0).astype(BF16)
            qp[at, vcols] = dv[at, :].astype(BF16)

    transfers("attb0", (attend_back, 0))

    def pool_is_free():
        pl.semaphore_signal(free, inc=1, device_id=who["core"], device_id_type=MESH)

    transfers("attb1", (attend_back, 1), (pool_is_free,))
    for c in range(CHUNKS):
        transfers(f"p2.{c}", (spread_columns, qp, win, y, r2, c))
    transfers("pool", (pl.semaphore_wait, free, 1))

    def mix_rows(at, with_pair):
        branches = total(p1, f1, a1, at, with_pair)
        mixed[at, :] = (tokens[at, :].astype(F32) + branches + (bo[...] + b2[...])).astype(BF16)

    @step
    def mix():
        for c in range(CHUNKS):
            r1(c).arrived()
        each_row_block(mix_rows)
        send_out(0, *outputs[0])

    @step
    def bias():
        def part(i, carry):
            at = rows_at(i * 128, 128)
            sums = jnp.sum(qp[at, :].astype(F32), axis=0, keepdims=True)
            small[6:7, :] += sums[:, 0:1024]
            small[7:8, 0:QKV] += sums[:, 1024:IN_W]
            return carry

        small[...] = jnp.zeros_like(small)
        lax.fori_loop(0, 8, part, 0)

    def norm_of(at):
        values = tokens[at, :].astype(F32)
        center = values - jnp.mean(values, axis=-1, keepdims=True)
        rstd = lax.rsqrt(jnp.mean(center * center, axis=-1, keepdims=True) + 1e-05)
        return center * rstd, rstd

    def sums_of(at, with_pair):
        ngrad = total(y, f2, a2, at, with_pair)
        for n, term in enumerate((ngrad * norm_of(at)[0], ngrad, cot[at, :].astype(F32))):
            sums = jnp.sum(term, axis=0, keepdims=True)
            small[2 * n : 2 * n + 1, :] += sums[:, 0:1024]
            small[2 * n + 1 : 2 * n + 2, :] += sums[:, 1024:2048]

    def around(n, buffer, here, names, places):
        buffer[here] = small[...]
        copies = []
        for k, name in enumerate(names):
            i = n + k
            copies.append(remote(buffer.at[here], buffer.at[here], sms.at[i], smr.at[i], who[name]))
            copies[-1].start()

        def finish():
            for k, name in enumerate(names):
                there = buffer.at[places[k]]
                remote(there, there, sms.at[n + k], smr.at[n + k], who[name]).wait_recv()
            for c in copies:
                c.wait_send()

        return finish

    xi = xh * 2 + xl
    along_x = [((xi + way) % 4) * 2 for way in (3, 1, 2)]
    rounds = {}

    @step
    def sums():
        for c in range(CHUNKS):
            r2(c).arrived()
        each_row_block(sums_of)
        rounds["x"] = around(
            0,
            got_x,
            xi * 2 + core,
            ("core", "xp", "xm", "xx", "xp2", "xm2", "xx2"),
            [xi * 2 + 1 - core] + [p + core for p in along_x] + [p + 1 - core for p in along_x],
        )

    def back_norm(at, with_pair):
        xhat, rstd = norm_of(at)
        ex = total(y, f2, a2, at, with_pair) * gain[...]
        mean_e = jnp.mean(ex, axis=-1, keepdims=True)
        mean_ex = jnp.mean(ex * xhat, axis=-1, keepdims=True)
        tgrad[at, :] = (cot[at, :].astype(F32) + (ex - mean_e - xhat * mean_ex) * rstd).astype(BF16)

    transfers("back", (each_row_block, back_norm), (send_out, 1, *outputs[1]))

    @step
    def sum_x():
        rounds["x"]()
        small[0:6, :] = jnp.sum(got_x[:, 0:6, :], axis=0)
        small[6:8, :] = jnp.sum(got_x[pl.ds(4 * xh, 4), 6:8, :], axis=0)
        rounds["z"] = around(7, got.at[0], z, ("zp", "zm", "zz"), [(z + way) % 4 for way in (3, 1, 2)])

    @step
    def sum_z():
        rounds["z"]()
        small[...] = jnp.sum(got[0], axis=0)
        rounds["y"] = around(10, got.at[1], yy, ("yp", "ym", "yy"), [(yy + way) % 4 for way in (3, 1, 2)])

    @step
    def sum_y():
        rounds["y"]()
        small[0:6, :] = jnp.sum(got[1, :, 0:6, :], axis=0)

    @step
    def lasto():
        def rows(at):
            gout[at, :] = ro.total(at)

        ro.arrived()
        each(ROWS, rows)
        send_out(3, *outputs[3])

    @step
    def lastf():
        def rows(at):
            gin[at, QKV:IN_W] = rf.total(at)

        rf.arrived()
        each(ROWS, rows)

    @step
    def lastq():
        def rows(at):
            gin[at, 0:QKV] = rq.total(at)

        rq.arrived()
        each(ROWS, rows)

    for name in ORDER:
        steps[name]()
    send_out(2, *outputs[2])
    send_out(4, *outputs[4])

    for c in range(CHUNKS):
        r1(c).sent()
        r2(c).sent()
    for r in (ro, rf, rq):
        r.sent()
    for c in out_copies + fc_copies + qkv_copies:
        c.wait_send()
    for index, (src, dst) in enumerate(outputs):
        pltpu.make_async_copy(src, dst, out_of.at[index]).wait()


def block(*args):
    sems = pltpu.SemaphoreType.DMA

    def low(*shape):
        return pltpu.VMEM(shape, BF16)

    ring = [low(2, ROWS, D), low(2, 2, ROWS, D), low(KEEP, D), low(4, ROWS - KEEP, D)]
    rows_4d = low(4, 2, ROWS, D)
    smem = pl.BlockSpec(memory_space=pltpu.SMEM)
    return pl.pallas_call(
        block_kernel,
        out_shape=(
            jax.ShapeDtypeStruct((ROWS, D), BF16),
            jax.ShapeDtypeStruct((ROWS, D), BF16),
            jax.ShapeDtypeStruct((ROWS, IN_W), F32),
            jax.ShapeDtypeStruct((ROWS, OUT_W), F32),
            jax.ShapeDtypeStruct((8, 1024), F32),
        ),
        in_specs=[ANY, ANY, smem, ANY, VMEM, ANY, VMEM, ANY, VMEM, ANY] + [VMEM] * 5,
        out_specs=(ANY,) * 5,
        scratch_shapes=[
            low(ROWS, D), low(ROWS, D), low(256, ROWS), low(FC, ROWS),
            pltpu.VMEM((ROWS, IN_W), F32), pltpu.VMEM((ROWS, OUT_W), F32), pltpu.VMEM((8, 1024), F32),
            sems((9,)), sems((5,)),
            low(GROUP, D), rows_4d, low(D, IN_W), low(D, OUT_W),
            low(GROUP, OUT_W), low(GROUP, IN_W), low(GROUP, 256), low(2560, GROUP), rows_4d,
            pltpu.VMEM((GROUP, 128), F32), pltpu.VMEM((GROUP, 128), F32),
            pltpu.VMEM((GROUP, 128), F32), pltpu.VMEM((GROUP, 128), F32),
            *ring, *ring,
            low(2, ROWS, IN_W), low(2, 2, ROWS, IN_W), low(ROWS, IN_W),
            low(2, ROWS, OUT_W), low(2, 2, ROWS, OUT_W), low(ROWS, OUT_W),
            low(8 * ROWS, OUT_W),
            pltpu.VMEM((8, 8, 1024), F32), pltpu.VMEM((2, 4, 8, 1024), F32),
            low(256, GROUP), low(256, GROUP),
            sems((12,)), sems((12,)), sems((12,)), sems((12,)),
            sems((9,)), sems((9,)), sems((10,)), sems((10,)),
            sems((9,)), sems((9,)), sems((10,)), sems((10,)),
            sems((CHUNKS, 8)), sems((CHUNKS, 8)), sems((CHUNKS, 8)), sems((CHUNKS, 8)),
            sems((7,)), sems((7,)), sems((7,)), sems((7,)), sems((7,)), sems((7,)),
            sems((8,)), sems((8,)), sems((8,)), sems((8,)), sems((8,)), sems((8,)),
            sems((13,)), sems((13,)), pltpu.SemaphoreType.REGULAR,
        ],
        compiler_params=pltpu.CompilerParams(
            collective_id=0, has_side_effects=True, vmem_limit_bytes=VMEM_LIMIT
        ),
        name="block",
    )(*args)


def finish_kernel(
    mixed, tgrad, gin, gout, small,
    o_mixed, o_tgrad, gq, bq, go, bo, g1, b1, g2, b2, gain, shift,
    kept, sums, sem,
):
    def copy(index, src, dst):
        c = pltpu.make_async_copy(src, dst, sem.at[index])
        c.start()
        return c

    out, totals = copy(0, gout, kept), copy(1, small, sums)
    rest = [copy(2, mixed, o_mixed), copy(3, tgrad, o_tgrad), copy(4, gin.at[:, QKV:IN_W], g1)]
    for t in range(3):
        rest.append(copy(5 + t, gin.at[:, t * 256 : (t + 1) * 256], gq.at[t]))
    totals.wait()
    for t in range(3):
        bq[t : t + 1, :] = sums[6:7, t * 256 : (t + 1) * 256]
    b1[:, 0:256] = sums[6:7, QKV:1024]
    b1[:, 256:FC] = sums[7:8, 0:QKV]
    for n in range(2):
        cols = slice(n * 1024, (n + 1) * 1024)
        gain[:, cols] = sums[n : n + 1, :]
        shift[:, cols] = sums[2 + n : 3 + n, :]
        bo[:, cols] = sums[4 + n : 5 + n, :]
        b2[:, cols] = sums[4 + n : 5 + n, :]
    out.wait()
    go[...] = kept[:, 0:256].T
    for j in range(8):
        g2[j * 128 : (j + 1) * 128, :] = kept[:, 256 + j * 128 : 256 + (j + 1) * 128].T
    for c in rest:
        c.wait()


def finish(*args):
    def out(*shape):
        return jax.ShapeDtypeStruct(shape, F32)

    rows = jax.ShapeDtypeStruct((ROWS, D), BF16)
    shapes = (
        rows, rows, out(3, ROWS, 256), out(3, 256), out(256, ROWS), out(1, D), out(ROWS, FC), out(1, FC),
        out(FC, ROWS), out(1, D), out(1, D), out(1, D),
    )
    return pl.pallas_call(
        finish_kernel,
        out_shape=shapes,
        in_specs=[ANY] * 5,
        out_specs=(VMEM,) * 12,
        scratch_shapes=[
            pltpu.VMEM((ROWS, OUT_W), F32), pltpu.VMEM((8, 1024), F32), pltpu.SemaphoreType.DMA((8,))
        ],
        compiler_params=pltpu.CompilerParams(vmem_limit_bytes=VMEM_LIMIT),
        name="finish",
    )(*args)


def per_device(
    tokens, cotangent, seq_lengths, w_qkv, b_qkv, w_out, b_out, w_fc1, b_fc1, w_fc2, b_fc2, ln_gain, ln_bias
):
    lane = np.arange(128) % HD
    angle = np.float32(10000.0) ** (np.float32(-2.0) * (lane % (ROT // 2)).astype(np.float32) / np.float32(ROT))
    freq = jnp.asarray(np.where(lane < ROT, angle, 0.0).astype(np.float32))
    sign = jnp.asarray(np.where(lane < ROT // 2, -1.0, np.where(lane < ROT, 1.0, 0.0)).astype(np.float32))
    parts = block(
        tokens, cotangent, seq_lengths, jnp.transpose(w_qkv, (1, 0, 2)), b_qkv, w_out, b_out[None], w_fc1,
        b_fc1[None], w_fc2, b_fc2[None], ln_gain[None], ln_bias[None], freq[None], sign[None],
    )
    mixed, tgrad, gq, bq, go, bo, g1, b1, g2, b2, gain, shift = finish(*parts)
    return (
        mixed, tgrad, jnp.transpose(gq, (1, 0, 2)), bq, go, bo[0], g1, b1[0], g2, b2[0], gain[0], shift[0]
    )


def solution(mesh):
    in_specs = (
        P(("dp", "mp"), None),
        P(("dp", "mp"), None),
        P("dp", None),
        P("dp", None, "mp"),
        P(None, "mp"),
        P("mp", "dp"),
        P(),
        P("dp", "mp"),
        P("mp"),
        P("mp", "dp"),
        P(),
        P(),
        P(),
    )
    out_specs = (
        P(("dp", "mp"), None),
        P(("dp", "mp"), None),
        P("dp", None, "mp"),
        P(None, "mp"),
        P("mp", "dp"),
        P(),
        P("dp", "mp"),
        P("mp"),
        P("mp", "dp"),
        P(),
        P(),
        P(),
    )
    return jax.shard_map(
        per_device, mesh=mesh, in_specs=in_specs, out_specs=out_specs, check_vma=False
    )
```

time: 690 us -> 187 us (0.27); the launches traced: 680 us -> 187 us
  waiting for transfers between devices: 299 us -> 0 us
  Pallas kernels: 0 us -> 186 us
  blocking collectives: 147 us -> 0 us
  matrix products: 113 us -> 0 us
  local copies, waits for them, and re-layouts: 45.5 us -> 0 us
  other arithmetic: 38.9 us -> 0 us
  starting transfers between devices: 20.5 us -> 0 us
  between operations: 15.2 us -> 0.84 us
    all_gather x6 -> x0, waiting for transfers between devices: 210 us -> none  [the longest x1 73.6 us: per_device(): lax.all_gather(normed.astype(jnp.bfloat16), 'mp', axis=0, tiled=True)]
    pallas_call x0 -> x2, Pallas kernels: none -> 186 us  [the longest x1 183 us: block(): pl.pallas_call(block_kernel, out_shape=(jax.ShapeDtypeStruct((ROWS, D), B...]
    psum x2 -> x0, blocking collectives: 147 us -> none  [the longest x1 82.5 us: per_device(): qkv_bias_sum, up_bias_sum = lax.psum((qkv_bias_grad, up_bias_grad), 'dp')]
    dot_general x26 -> x0, matrix products: 113 us -> none  [the longest x1 11.7 us: per_device(): jnp.einsum('gd,fd->gf', grads_all, down_full, preferred_element_type=jnp....]
    all_to_all x4 -> x0, waiting for transfers between devices: 86.8 us -> none  [summed_on_arrival(): lax.all_to_all(tiles, axis, split_axis=0, concat_axis=0, tiled=True)]
    reduce_sum x14 -> x0, other arithmetic: 25.9 us -> none  [the longest x4 10.9 us: summed_on_arrival(): return arrived.astype(jnp.float32).sum(axis=0)]
    dynamic_update_slice x8 -> x0, local copies, waits for them, and re-layouts: 23.6 us -> none  [the longest x4 21.9 us: per_device(): lax.scan(backward_block, (zero_heads, zero_heads), (query_blocks, seg_blo...]
    all_to_all x4 -> x0, starting transfers between devices: 20.2 us -> none  [summed_on_arrival(): lax.all_to_all(tiles, axis, split_axis=0, concat_axis=0, tiled=True)]
  transfers between devices with their start and end apart: 12 -> 0, of which waited for: 7 -> 0; matrix products, arithmetic and copies ran while one was open for 25% -> 0% of each run, Pallas kernels for 0% -> 0%
where the time goes in v1:
time: 187 us
  Pallas kernels  186 us (99%)
    pallas_call x1, Pallas kernels, block(): pl.pallas_call(block_kernel, out_shape=(jax.ShapeDtypeStruct((ROWS, D), B...  183 us

profile of v1, /device:TPU:1, one launch (start us, length us, event | category | flops | bytes accessed | tf_op | source)
XLA Modules:
  0.0 186.7 jit_solution(6373536787458414404)
XLA Ops:
  0.6 182.6 %block.1 = (bf16[128,2048]{1,0:T(8,128)(2,1)}, bf16[128,2048]{1,0:T(8,128)(2,1)}, f32[128,1792]{1,0:T(8,128)}, f32[128,1280]{1,0:T(8,128)}, f32[8,1024]{1,0:T(8,128)}) custom-call(bf16[128,2048]{1,0:T(8,128)(2,1)} %tokens_in.1, bf16[128,2048]{1,0:T(8,128)(2,1)} %cot_in.1, s32[1,4]{1,0:T(1,128)} %lens.1, bf16[3,128,256]{2,1,0:T(8,128)(2,1)} %bitcast.12, ...), custom_call_target="tpu_custom_call" | custom-call | tf_op jit(solution)/shard_map/block/pallas_call | solution.py:875
  183.2 3.2 %finish.1 = (bf16[128,2048]{1,0:T(8,128)(2,1)}, bf16[128,2048]{1,0:T(8,128)(2,1)}, f32[3,128,256]{2,1,0:T(8,128)}, f32[3,256]{1,0:T(4,128)}, f32[256,128]{1,0:T(...) custom-call(bf16[128,2048]{1,0:T(8,128)(2,1)} %get-tuple-element.29., ...), custom_call_target="tpu_custom_call" | custom-call | tf_op jit(solution)/shard_map/finish/pallas_call | solution.py:957

commit v2 on v1

--- a/solution.py
+++ b/solution.py
@@ -36,7 +36,7 @@
     "dwi0", "dwi1", "mix", "r20_s1a", "r21_qa", "kq.t0", "dwi2", "r22_qa", "kf.t0", "kf.t1", "r23_qa", "kq.t1",
     "dwi3", "kq.t2", "kf.t2", "rq.s1b", "rq.s1a", "r20_th", "r22_s1b", "r21_s1a", "kq.t3", "kf.t3", "r22_s1a",
     "r21_th", "r23_s1a", "r23_s1b", "r22_th", "rf.s1b", "r23_th", "rf.s1a", "sums", "rq.th", "lasto", "back",
-    "sum_x", "sum_z", "lastq", "rf.th", "sum_y", "lastf",
+    "rf.th", "sum_x", "sum_z", "sum_y", "lastq", "lastf",
 )
 
 VMEM = pl.BlockSpec(memory_space=pltpu.VMEM)

time: 187 us -> 183 us (0.979)
  Pallas kernels: 186 us -> 182 us
    pallas_call x1, Pallas kernels: 183 us -> 179 us  [block(): pl.pallas_call(block_kernel, out_shape=(jax.ShapeDtypeStruct((ROWS, D), B...]
where the time goes in v2:
time: 183 us
  Pallas kernels  182 us (99%)
    pallas_call x1, Pallas kernels, block(): pl.pallas_call(block_kernel, out_shape=(jax.ShapeDtypeStruct((ROWS, D), B...  179 us

profile of v2, /device:TPU:1, one launch (start us, length us, event | category | flops | bytes accessed | tf_op | source)
XLA Modules:
  0.0 182.8 jit_solution(16432113510159212572)
XLA Ops:
  0.6 178.7 %block.1 = (bf16[128,2048]{1,0:T(8,128)(2,1)}, bf16[128,2048]{1,0:T(8,128)(2,1)}, f32[128,1792]{1,0:T(8,128)}, f32[128,1280]{1,0:T(8,128)}, f32[8,1024]{1,0:T(8,128)}) custom-call(bf16[128,2048]{1,0:T(8,128)(2,1)} %tokens_in.1, bf16[128,2048]{1,0:T(8,128)(2,1)} %cot_in.1, s32[1,4]{1,0:T(1,128)} %lens.1, bf16[3,128,256]{2,1,0:T(8,128)(2,1)} %bitcast.12, ...), custom_call_target="tpu_custom_call" | custom-call | tf_op jit(solution)/shard_map/block/pallas_call | solution.py:875
  179.4 3.2 %finish.1 = (bf16[128,2048]{1,0:T(8,128)(2,1)}, bf16[128,2048]{1,0:T(8,128)(2,1)}, f32[3,128,256]{2,1,0:T(8,128)}, f32[3,256]{1,0:T(4,128)}, f32[256,128]{1,0:T(...) custom-call(bf16[128,2048]{1,0:T(8,128)(2,1)} %get-tuple-element.29., ...), custom_call_target="tpu_custom_call" | custom-call | tf_op jit(solution)/shard_map/finish/pallas_call | solution.py:957
